TPU v7x, 32 devices: a whole 2x2x4 slice. The times are simulated.
32 devices in a mesh: cells: 32 (over z, y, x, core).
Axes of the slice: x: 2, y: 2, z: 4, core: 2. Of those that a mesh axis runs over, the one named last changes fastest.
Arguments:
- multipoles: bfloat16 [216, 32768], P(None, 'cells'), may hold values from -6 to 6
- compress: bfloat16 [216, 128], replicated, may hold values from -0.4375 to 0.4375
- operators: bfloat16 [316, 128, 128], replicated, may hold values from -0.0390625 to 0.0390625
- expand: bfloat16 [128, 216], replicated, may hold values from -0.5 to 0.5
Outputs:
- local_field: float32 [216, 32768], P(None, 'cells')
All inputs are finite; a program needn't handle non-finite values.
Results may differ from a plain program's by a relative error of at most 0.0041.
Values may be sent and summed in bfloat16 or wider, within the bound.
A program may use at most 256 MiB of HBM per device.

v0:
```python
import functools

import jax
import jax.numpy as jnp
import numpy as np
from jax import lax
from jax.experimental import pallas as pl
from jax.experimental.pallas import tpu as pltpu
from jax.sharding import PartitionSpec as P

SIDE = (8, 4, 4)
PLANE = SIDE[1] * SIDE[2]
FLAT = [(0, 1, 0), (0, -1, 0), (0, 0, 1), (0, 0, -1), (0, 1, 1), (0, 1, -1), (0, -1, 1), (0, -1, -1)]
SLANT = [(ex, ey, ez) for ex in (-1, 1) for ey in (-1, 0, 1) for ez in (-1, 0, 1)]
WAYS = FLAT + SLANT


def slot_table():
    table, start = {}, 0
    for way in WAYS:
        rows = 32 if way in FLAT[:4] else 16
        table[way] = (start, rows)
        start += rows
    return table, start


SLOTS, SLOT_ROWS = slot_table()
FLAT_ROWS = SLOTS[SLANT[0]][0]


def offset_table():
    table = {}
    for sx in range(-3, 4):
        for sy in range(-3, 4):
            for sz in range(-3, 4):
                if max(abs(sx), abs(sy), abs(sz)) >= 2:
                    table[(sx, sy, sz)] = len(table)
    return table


def parent_place(morton):
    coords = [0, 0, 0]
    for bit in range(7):
        coords[bit % 3] += (morton >> bit & 1) << (bit // 3)
    return (coords[0] * SIDE[1] + coords[1]) * SIDE[2] + coords[2]


def picks():
    table = np.zeros((SIDE[0] + 2, 9 * PLANE, 256), np.float32)
    for plane in range(SIDE[0] + 2):
        x = plane - 1
        row = 0
        for dz in (-1, 0, 1):
            for dy in (-1, 0, 1):
                for y in range(SIDE[1]):
                    for z in range(SIDE[2]):
                        sy, sz = y + dy, z + dz
                        ey = -1 if sy < 0 else 1 if sy >= SIDE[1] else 0
                        ez = -1 if sz < 0 else 1 if sz >= SIDE[2] else 0
                        wy, wz = sy % SIDE[1], sz % SIDE[2]
                        if x < 0 or x >= SIDE[0]:
                            block = (ey + 1) * 3 + ez + 1
                            column = block * PLANE + wy * SIDE[2] + wz
                        elif ey == 0 and ez == 0:
                            column = FLAT_ROWS + wy * SIDE[2] + wz
                        else:
                            start = SLOTS[(0, ey, ez)][0]
                            line = wz if ez == 0 else wy if ey == 0 else 0
                            column = start + line * SIDE[0] + x
                        table[plane, row, column] = 1
                        row += 1
    return table


def bits_of_dimension(device_count, local_bits):
    count = device_count.bit_length() - 1
    return [[bit for bit in range(count) if (local_bits + bit) % 3 == dim] for dim in range(3)]


def exchange_kernel(bit_lists, multipoles, compress, own, recv, field, send, send_sem, recv_sem):
    me = lax.axis_index("cells")
    position = []
    for bits in bit_lists:
        value = me * 0
        for rank, bit in enumerate(bits):
            value = value + (me // 2**bit) % 2 * 2**rank
        position.append(value)

    def neighbour(way):
        inside, device = None, me * 0
        for dim, bits in enumerate(bit_lists):
            place = position[dim] + way[dim]
            if way[dim]:
                fits = (place >= 0) & (place < 2 ** len(bits))
                inside = fits if inside is None else inside & fits
            for rank, bit in enumerate(bits):
                device = device + (place + 2 ** len(bits)) // 2**rank % 2 * 2**bit
        return inside, device

    ways = [way for way in WAYS if all(bits or not step for bits, step in zip(bit_lists, way))]
    near = {way: neighbour(way) for way in ways}
    barrier = pltpu.get_barrier_semaphore()
    for way in ways:
        inside, device = near[way]

        @pl.when(inside)
        def _():
            pl.semaphore_signal(barrier, inc=1, device_id=(device,), device_id_type=pl.DeviceIdType.MESH)

    compressed = lax.dot_general(
        multipoles[...], compress[...], (((0,), (0,)), ((), ())), preferred_element_type=jnp.float32
    )
    compressed = compressed.astype(jnp.bfloat16).astype(jnp.float32)
    for morton in range(SIDE[0] * PLANE):
        place = parent_place(morton)
        field[place * 8 : place * 8 + 8, :] = compressed[morton * 8 : morton * 8 + 8, :]

    def lanes(child):
        cx, cy, cz = child & 1, child >> 1 & 1, child >> 2
        start = (cx * 4 + cy * 2 + cz) * 128
        return slice(start, start + 128)

    for child in range(8):
        for x in range(SIDE[0]):
            rows = field[pl.ds(x * PLANE * 8 + child, PLANE, stride=8), :]
            own[x * PLANE : (x + 1) * PLANE, lanes(child)] = rows.astype(jnp.bfloat16)

    def column(y, z, child):
        return field[pl.ds((y * SIDE[2] + z) * 8 + child, SIDE[0], stride=PLANE * 8), :]

    for way in FLAT:
        start, rows = SLOTS[way]
        y = SIDE[1] - 1 if way[1] > 0 else 0
        z = SIDE[2] - 1 if way[2] > 0 else 0
        for child in range(8):
            if way[2] == 0:
                parts = [column(y, line, child) for line in range(SIDE[2])]
            elif way[1] == 0:
                parts = [column(line, z, child) for line in range(SIDE[1])]
            else:
                parts = [column(y, z, child)]
                parts.append(jnp.zeros_like(parts[0]))
            packed = jnp.concatenate(parts, axis=0).astype(jnp.bfloat16)
            send[start : start + rows, lanes(child)] = packed

    peers = me * 0
    for way in ways:
        peers = peers + jnp.where(near[way][0], 1, 0)
    pl.semaphore_wait(barrier, peers)

    def copy_to(way):
        start, rows = SLOTS[way]
        back = tuple(-step for step in way)
        target = SLOTS[back][0]
        if way[0]:
            x = SIDE[0] - 1 if way[0] > 0 else 0
            source = own.at[pl.ds(x * PLANE, PLANE)]
        else:
            source = send.at[pl.ds(start, rows)]
        return pltpu.make_async_remote_copy(
            src_ref=source,
            dst_ref=recv.at[pl.ds(target, rows)],
            send_sem=send_sem.at[WAYS.index(way)],
            recv_sem=recv_sem.at[WAYS.index(back)],
            device_id=(near[way][1],),
            device_id_type=pl.DeviceIdType.MESH,
        )

    for way in ways:

        @pl.when(near[way][0])
        def _():
            copy_to(way).start()

    for way in WAYS:
        start, rows = SLOTS[way]
        blank = jnp.zeros((rows, recv.shape[1]), recv.dtype)
        if way in near:

            @pl.when(jnp.logical_not(near[way][0]))
            def _():
                recv[start : start + rows, :] = blank
        else:
            recv[start : start + rows, :] = blank

    for way in ways:
        back = tuple(-step for step in way)

        @pl.when(near[way][0])
        def _():
            copy_to(way).wait_send()
            copy_to(back).wait_recv()


def interact_kernel(own, recv, pick, expand, operators, out, held, spread, total, flat, load_sem):
    offsets = offset_table()
    spans = {}
    for (sx, _, _), number in offsets.items():
        low, high = spans.get(sx, (number, number))
        spans[sx] = (min(low, number), max(high, number))

    def load(sx):
        low, high = spans[sx]
        rows = pl.ds(low, high - low + 1)
        return pltpu.make_async_copy(operators.at[rows], held.at[rows], load_sem.at[sx + 3])

    for sx in range(-3, 4):
        load(sx).start()

    for plane in range(SIDE[0] + 2):
        if 1 <= plane <= SIDE[0]:
            parts = [(recv, 0, FLAT_ROWS), (own, (plane - 1) * PLANE, PLANE)]
        else:
            parts = [(recv, SLOTS[SLANT[0 if plane == 0 else 9]][0], 9 * PLANE)]
        used = sum(part[2] for part in parts)
        for pair in range(4):
            lanes = slice(pair * 256, pair * 256 + 256)
            values = [ref[start : start + rows, lanes] for ref, start, rows in parts]
            values.append(jnp.zeros((256 - used, 256), jnp.bfloat16))
            copies = jnp.dot(
                pick[plane], jnp.concatenate(values, axis=0), preferred_element_type=jnp.float32
            ).astype(jnp.bfloat16)
            for dz in range(3):
                for dy in range(3):
                    row = (dz * 3 + dy) * PLANE
                    spread[pair, dy, plane, :, dz * 256 : dz * 256 + 256] = copies[row : row + PLANE, :]

    total[...] = jnp.zeros_like(total)
    for sx in range(-3, 4):
        load(sx).wait()
        for sy in range(-3, 4):
            weights, shifts = [], []
            for dz in (-1, 0, 1):
                lines = []
                for cz in (0, 1):
                    entries = []
                    for pz in (0, 1):
                        number = offsets.get((sx, sy, 2 * dz + cz - pz))
                        entries.append(None if number is None else held[number])
                    lines.append(entries)
                if all(entry is None for line in lines for entry in line):
                    continue
                blank = jnp.zeros((128, 128), jnp.bfloat16)
                for line in lines:
                    line = [blank if entry is None else entry for entry in line]
                    weights.append(jnp.concatenate(line, axis=1))
                shifts.append(dz + 1)
            weights = jnp.concatenate(weights, axis=0)
            classes, sources = [], []
            for px in (0, 1):
                for py in (0, 1):
                    dx, cx = (px + sx) // 2, (px + sx) % 2
                    dy, cy = (py + sy) // 2, (py + sy) % 2
                    if abs(dx) > 1 or abs(dy) > 1:
                        continue
                    source = spread[cx * 2 + cy, dy + 1, 1 + dx : 1 + dx + SIDE[0]]
                    source = source.reshape(SIDE[0] * PLANE, 768)
                    if len(shifts) < 3:
                        source = jnp.concatenate(
                            [source[:, dz * 256 : dz * 256 + 256] for dz in shifts], axis=1
                        )
                    classes.append(px * 2 + py)
                    sources.append(source)
            product = jnp.dot(
                jnp.concatenate(sources, axis=0), weights, preferred_element_type=jnp.float32
            )
            count = SIDE[0] * PLANE
            for number, kind in enumerate(classes):
                total[kind] += product[number * count : (number + 1) * count, :]

    for px in (0, 1):
        for py in (0, 1):
            for pz in (0, 1):
                child = px + 2 * py + 4 * pz
                rows = total[px * 2 + py, :, pz * 128 : pz * 128 + 128]
                flat[pl.ds(child, SIDE[0] * PLANE, stride=8), :] = rows
    places = [parent_place(morton) for morton in range(SIDE[0] * PLANE)]
    reduced = jnp.concatenate([flat[place * 8 : place * 8 + 8, :] for place in places], axis=0)
    out[...] = lax.dot_general(
        expand[...].T, reduced.astype(jnp.bfloat16), (((1,), (1,)), ((), ())),
        preferred_element_type=jnp.float32,
    )


def local(multipoles, compress, operators, expand):
    cells, rank = multipoles.shape[1], compress.shape[1]
    devices = lax.axis_size("cells")
    local_bits = cells.bit_length() - 1
    bit_lists = bits_of_dimension(devices, local_bits)
    vmem = pl.BlockSpec(memory_space=pltpu.VMEM)
    parents = SIDE[0] * PLANE
    own, recv = pl.pallas_call(
        functools.partial(exchange_kernel, bit_lists),
        out_shape=[
            jax.ShapeDtypeStruct((parents, 8 * rank), jnp.bfloat16),
            jax.ShapeDtypeStruct((SLOT_ROWS, 8 * rank), jnp.bfloat16),
        ],
        in_specs=[vmem] * 2,
        out_specs=[vmem] * 2,
        scratch_shapes=[
            pltpu.VMEM((cells, rank), jnp.float32),
            pltpu.VMEM((FLAT_ROWS, 8 * rank), jnp.bfloat16),
            pltpu.SemaphoreType.DMA((len(WAYS),)),
            pltpu.SemaphoreType.DMA((len(WAYS),)),
        ],
        compiler_params=pltpu.CompilerParams(
            collective_id=0, has_side_effects=True, vmem_limit_bytes=24 * 2**20
        ),
        name="halo_exchange",
    )(multipoles, compress)
    return pl.pallas_call(
        interact_kernel,
        out_shape=jax.ShapeDtypeStruct((expand.shape[1], cells), jnp.float32),
        in_specs=[vmem] * 4 + [pl.BlockSpec(memory_space=pl.ANY)],
        out_specs=vmem,
        scratch_shapes=[
            pltpu.VMEM(operators.shape, jnp.bfloat16),
            pltpu.VMEM((4, 3, SIDE[0] + 2, PLANE, 6 * rank), jnp.bfloat16),
            pltpu.VMEM((4, parents, 2 * rank), jnp.float32),
            pltpu.VMEM((cells, rank), jnp.float32),
            pltpu.SemaphoreType.DMA((7,)),
        ],
        compiler_params=pltpu.CompilerParams(vmem_limit_bytes=48 * 2**20),
        name="interactions",
    )(own, recv, jnp.asarray(picks(), jnp.bfloat16), expand, operators)


def solution(mesh):
    placed = (P(None, "cells"), P(), P(), P())
    return jax.shard_map(
        local, mesh=mesh, in_specs=placed, out_specs=P(None, "cells"), check_vma=False
    )
```

profile of v0, /device:TPU:7, one launch (start us, length us, event | category | flops | bytes accessed | tf_op | source)
XLA Modules:
  0.0 35.0 jit_solution(12599248388908219847)
XLA Ops:
  0.0 0.9 %copy.6.expand = bf16[128,216]{1,0:T(8,128)(2,1)S(1)} copy(bf16[128,216]{0,1:T(8,128)(2,1)} %param.8) | data formatting | bytes 110592 | tf_op args[3]
  0.9 0.0 copy-start.1
  0.9 1.0 %copy-done.1 = bf16[216,1024]{1,0:T(8,128)(2,1)S(1)} copy-done((bf16[216,1024]{1,0:T(8,128)(2,1)S(1)}, bf16[216,1024]{1,0:T(8,128)(2,1)}, u32[]{:S(2)}) %copy-start.1) | copy-done | bytes 442392
  1.9 0.0 copy-start.2
  1.9 0.8 %copy-done.2 = bf16[216,128]{1,0:T(8,128)(2,1)S(1)} copy-done((bf16[216,128]{1,0:T(8,128)(2,1)S(1)}, bf16[216,128]{1,0:T(8,128)(2,1)}, u32[]{:S(2)}) %copy-start.2) | copy-done | bytes 55320
  2.7 15.0 %halo_exchange.1 = (bf16[128,1024]{1,0:T(8,128)(2,1)S(1)}, bf16[480,1024]{1,0:T(8,128)(2,1)S(1)}) custom-call(bf16[216,1024]{1,0:T(8,128)(2,1)S(1)} %copy-done.1, bf16[216,128]{1,0:T(8,128)(2,1)S(1)} %copy-done.2), custom_call_target="tpu_custom_call" | custom-call | tf_op jit(solution)/shard_map/halo_exchange/pallas_call | solution.py:292
  17.8 0.0 copy-start
  17.8 1.1 %copy-done = bf16[10,144,256]{2,1,0:T(8,128)(2,1)S(1)} copy-done((bf16[10,144,256]{2,1,0:T(8,128)(2,1)S(1)}, bf16[10,144,256]{2,1,0:T(8,128)(2,1)}, u32[]{:S(2)}) %copy-start) | copy-done | bytes 737304
  18.9 16.1 %interactions.1 = f32[216,1024]{1,0:T(8,128)} custom-call(bf16[128,1024]{1,0:T(8,128)(2,1)S(1)} %get-tuple-element.7.own, bf16[480,1024]{1,0:T(8,128)(2,1)S(1)} %get-tuple-element.8.recv, bf16[10,144,256]{2,1,0:T(8,128)(2,1)S(1)} %copy-done, bf16[128,216]{1,0:T(8,128)(2,1)S(1)} %copy.6.expand, bf16[316,128,128]{2,1,0:T(8,128)(2,1)} %operators.1), custom_call_target="tpu_custom_call" | custom-call | tf_op jit(solution)/shard_map/interactions/pallas_call | solution.py:311
Async XLA Ops:
  0.9 1.0 %copy-start.1 = (bf16[216,1024]{1,0:T(8,128)(2,1)S(1)}, bf16[216,1024]{1,0:T(8,128)(2,1)}, u32[]{:S(2)}) copy-start(bf16[216,1024]{1,0:T(8,128)(2,1)} %multipoles.1) | copy-start | bytes 1327108
  1.9 0.8 %copy-start.2 = (bf16[216,128]{1,0:T(8,128)(2,1)S(1)}, bf16[216,128]{1,0:T(8,128)(2,1)}, u32[]{:S(2)}) copy-start(bf16[216,128]{1,0:T(8,128)(2,1)} %compress.1) | copy-start | bytes 165892
  17.8 1.1 %copy-start = (bf16[10,144,256]{2,1,0:T(8,128)(2,1)S(1)}, bf16[10,144,256]{2,1,0:T(8,128)(2,1)}, u32[]{:S(2)}) copy-start(bf16[10,144,256]{2,1,0:T(8,128)(2,1)} %constant.2.clone.pick) | copy-start | bytes 2211844
where the time goes:
time: 35.3 us; the launch traced here: 35 us
  Pallas kernels  31.1 us (88%)
  local copies, waits for them, and re-layouts  3.84 us (11%)
    pallas_call x1, Pallas kernels, local(): pl.pallas_call(interact_kernel, out_shape=jax.ShapeDtypeStruct((expand.sh...  16.1 us
    pallas_call x1, Pallas kernels, local(): pl.pallas_call(functools.partial(exchange_kernel, bit_lists), out_shape=[...  15 us
    unnamed x7, local copies, waits for them, and re-layouts  3.84 us

commit v1 on v0

v1 whole, which is shorter than its diff:
```python
import functools

import jax
import jax.numpy as jnp
import numpy as np
from jax import lax
from jax.experimental import pallas as pl
from jax.experimental.pallas import tpu as pltpu
from jax.sharding import PartitionSpec as P

SIDE_X, SIDE_Y, SIDE_Z = SIDE = (8, 4, 4)
PLANE = SIDE_X * SIDE_Y
PARENTS = PLANE * SIDE_Z
WAYS = [
    (ex, ey, ez)
    for ez in (0, -1, 1)
    for ey in (-1, 0, 1)
    for ex in (-1, 0, 1)
    if (ex, ey, ez) != (0, 0, 0)
]
PLACES = {
    (-1, 0, 0): ("face", 0, 16),
    (1, 0, 0): ("face", 16, 16),
    (0, -1, 0): ("face", 32, 32),
    (0, 1, 0): ("face", 64, 32),
    (0, 0, -1): ("face", 96, 32),
    (0, 0, 1): ("face", 128, 32),
}
for way in WAYS:
    if way not in PLACES:
        kind = "edge" if way[0] == 0 else "thin"
        PLACES[way] = (kind, sum(place[0] == kind for place in PLACES.values()), 16)
PAIR_WAYS = [(ex, ey) for ey in (-1, 1) for ex in (-1, 1)]


def offset_table():
    table = {}
    for sx in range(-3, 4):
        for sy in range(-3, 4):
            for sz in range(-3, 4):
                if max(abs(sx), abs(sy), abs(sz)) >= 2:
                    table[(sx, sy, sz)] = len(table)
    return table


def parent_place(morton):
    coords = [0, 0, 0]
    for bit in range(7):
        coords[bit % 3] += (morton >> bit & 1) << (bit // 3)
    return (coords[2] * SIDE_Y + coords[1]) * SIDE_X + coords[0]


def picks():
    table = np.zeros((SIDE_Z + 2, 9 * PLANE, 256), np.float32)
    for plane in range(SIDE_Z + 2):
        z = plane - 1
        outer = z < 0 or z >= SIDE_Z
        row = 0
        for dy in (-1, 0, 1):
            for dx in (-1, 0, 1):
                for y in range(SIDE_Y):
                    for x in range(SIDE_X):
                        sy, sx = y + dy, x + dx
                        ey = -1 if sy < 0 else 1 if sy >= SIDE_Y else 0
                        ex = -1 if sx < 0 else 1 if sx >= SIDE_X else 0
                        wy, wx = sy % SIDE_Y, sx % SIDE_X
                        if ex == 0 and ey == 0:
                            column = wy * SIDE_X + wx
                        elif ex == 0:
                            column = 32 + (ey > 0) * 8 + wx if outer else 32 + (ey > 0) * 32 + z * 8 + wx
                        elif ey == 0:
                            column = 48 + (ex > 0) * 4 + wy if outer else 96 + (ex > 0) * 16 + z * 4 + wy
                        else:
                            corner = PAIR_WAYS.index((ex, ey))
                            column = 56 + corner if outer else 128 + corner * 4 + z
                        table[plane, row, column] = 1
                        row += 1
    return table


def bits_of_dimension(device_count, local_bits):
    count = device_count.bit_length() - 1
    return [[bit for bit in range(count) if (local_bits + bit) % 3 == dim] for dim in range(3)]


def reduce_kernel(
    bit_lists, multipoles_hbm, compress_hbm, pick_hbm, operators, out,
    multipoles, compress, pick, held, field, own, face_out, edge_out, thin_out,
    face_in, edge_in, thin_in, rim, spread, total, load_sem, send_sem, recv_sem,
):
    offsets = offset_table()
    spans = {}
    for (sx, _, _), number in offsets.items():
        low, high = spans.get(sx, (number, number))
        spans[sx] = (min(low, number), max(high, number))

    def load_operators(sx):
        low, high = spans[sx]
        rows = pl.ds(low, high - low + 1)
        return pltpu.make_async_copy(operators.at[rows], held.at[rows], load_sem.at[sx + 6])

    load_multipoles = pltpu.make_async_copy(multipoles_hbm, multipoles, load_sem.at[0])
    load_compress = pltpu.make_async_copy(compress_hbm, compress, load_sem.at[1])
    load_pick = pltpu.make_async_copy(pick_hbm, pick, load_sem.at[2])
    load_multipoles.start()
    load_compress.start()
    load_pick.start()
    for sx in range(-3, 4):
        load_operators(sx).start()

    me = lax.axis_index("cells")
    position = []
    for bits in bit_lists:
        value = me * 0
        for rank, bit in enumerate(bits):
            value = value + (me // 2**bit) % 2 * 2**rank
        position.append(value)

    def neighbour(way):
        inside, device = None, me * 0
        for dim, bits in enumerate(bit_lists):
            place = position[dim] + way[dim]
            if way[dim]:
                fits = (place >= 0) & (place < 2 ** len(bits))
                inside = fits if inside is None else inside & fits
            for rank, bit in enumerate(bits):
                device = device + (place + 2 ** len(bits)) // 2**rank % 2 * 2**bit
        return inside, device

    ways = [way for way in WAYS if all(bits or not step for bits, step in zip(bit_lists, way))]
    near = {way: neighbour(way) for way in ways}
    barrier = pltpu.get_barrier_semaphore()
    peers = me * 0
    for way in ways:
        inside, device = near[way]
        peers = peers + jnp.where(inside, 1, 0)

        @pl.when(inside)
        def _():
            pl.semaphore_signal(barrier, inc=1, device_id=(device,), device_id_type=pl.DeviceIdType.MESH)

    def slot(buffers, way):
        kind, start, rows = PLACES[way]
        if kind == "face":
            return buffers[0].at[pl.ds(start, rows)]
        return buffers[1 if kind == "edge" else 2].at[start]

    inboxes = (face_in, edge_in, thin_in)
    for way in WAYS:
        target = slot(inboxes, way)
        if way in near:

            @pl.when(jnp.logical_not(near[way][0]))
            def _():
                target[...] = jnp.zeros(target.shape, target.dtype)
        else:
            target[...] = jnp.zeros(target.shape, target.dtype)
    rim[...] = jnp.zeros_like(rim)

    load_multipoles.wait()
    load_compress.wait()
    compressed = lax.dot_general(
        multipoles[...], compress[...], (((0,), (0,)), ((), ())), preferred_element_type=jnp.float32
    )
    compressed = compressed.astype(jnp.bfloat16).astype(jnp.float32)
    for morton in range(PARENTS):
        place = parent_place(morton)
        field[place * 8 : place * 8 + 8, :] = compressed[morton * 8 : morton * 8 + 8, :]

    def child_of(cx, cy, cz):
        return cx + 2 * cy + 4 * cz

    def line(place, child, count, step):
        return field[pl.ds(place * 8 + child, count, stride=step * 8), :]

    def pack(parts):
        return jnp.concatenate(parts, axis=0).astype(jnp.bfloat16)

    children = [(cx, cy, cz) for cx in (0, 1) for cy in (0, 1) for cz in (0, 1)]
    for number, bits in enumerate(children):
        child, lanes = child_of(*bits), slice(number * 128, number * 128 + 128)
        for z in range(SIDE_Z):
            own[z * PLANE : (z + 1) * PLANE, lanes] = line(z * PLANE, child, PLANE, 1).astype(jnp.bfloat16)
        for ex in (-1, 1):
            start = PLACES[(ex, 0, 0)][1]
            x = SIDE_X - 1 if ex > 0 else 0
            face_out[start : start + 16, lanes] = line(x, child, 16, SIDE_X).astype(jnp.bfloat16)
        for ey in (-1, 1):
            start = PLACES[(0, ey, 0)][1]
            y = SIDE_Y - 1 if ey > 0 else 0
            parts = [line(z * PLANE + y * SIDE_X, child, SIDE_X, 1) for z in range(SIDE_Z)]
            face_out[start : start + 32, lanes] = pack(parts)
    for way in WAYS:
        kind, start, _ = PLACES[way]
        x = SIDE_X - 1 if way[0] > 0 else 0
        y = SIDE_Y - 1 if way[1] > 0 else 0
        z = SIDE_Z - 1 if way[2] > 0 else 0
        place = z * PLANE + y * SIDE_X + x
        if kind == "edge":
            for cy in (0, 1):
                for cz in (0, 1):
                    parts = [line(place, child_of(cx, cy, cz), SIDE_X, 1) for cx in (0, 1)]
                    edge_out[start, :, (cy * 2 + cz) * 128 : (cy * 2 + cz + 1) * 128] = pack(parts)
        elif kind == "thin":
            for cz in (0, 1):
                parts = []
                for pair in range(4):
                    child = child_of(pair // 2, pair % 2, cz)
                    if way[2] == 0:
                        parts.append(line(place, child, SIDE_Z, PLANE))
                    elif way[1] == 0:
                        parts.append(line(place, child, SIDE_Y, SIDE_X))
                    else:
                        parts.append(field[place * 8 + child : place * 8 + child + 1, :])
                if way[1] and way[2]:
                    parts.append(jnp.zeros((12, 128), jnp.float32))
                thin_out[start, :, cz * 128 : cz * 128 + 128] = pack(parts)

    pl.semaphore_wait(barrier, peers)

    def copy_to(way):
        back = tuple(-step for step in way)
        if way[:2] == (0, 0):
            source = own.at[pl.ds(PARENTS - PLANE if way[2] > 0 else 0, PLANE)]
        else:
            source = slot((face_out, edge_out, thin_out), way)
        return pltpu.make_async_remote_copy(
            src_ref=source,
            dst_ref=slot(inboxes, back),
            send_sem=send_sem.at[WAYS.index(way)],
            recv_sem=recv_sem.at[WAYS.index(back)],
            device_id=(near[way][1],),
            device_id_type=pl.DeviceIdType.MESH,
        )

    for way in ways:

        @pl.when(near[way][0])
        def _():
            copy_to(way).start()

    def arrive(way):
        @pl.when(near[way][0])
        def _():
            copy_to(tuple(-step for step in way)).wait_recv()

    def spread_plane(plane, pair, values):
        used = sum(value.shape[0] for value in values)
        values = jnp.concatenate(values + [jnp.zeros((256 - used, 256), jnp.bfloat16)], axis=0)
        copies = jnp.dot(pick[plane], values, preferred_element_type=jnp.float32)
        copies = copies.astype(jnp.bfloat16)
        for shift in range(9):
            spread[pair, shift, plane] = copies[shift * PLANE : (shift + 1) * PLANE, :]

    def thin_rows(way, pair, count):
        return thin_in[PLACES[way][1]].astype(jnp.float32)[pair * count : (pair + 1) * count, :]

    def interact(levels):
        for sx in range(-3, 4):
            if levels[0] != 0:
                load_operators(sx).wait()
            for sy in range(-3, 4):
                weights, shifts = [], []
                for dz in (-1, 0, 1):
                    entries = [
                        [offsets.get((sx, sy, 2 * dz + cz - pz)) for pz in (0, 1)] for cz in (0, 1)
                    ]
                    if all(entry is None for row in entries for entry in row):
                        continue
                    blank = jnp.zeros((128, 128), jnp.bfloat16)
                    for row in entries:
                        row = [blank if entry is None else held[entry] for entry in row]
                        weights.append(jnp.concatenate(row, axis=1))
                    shifts.append(dz)
                weights = jnp.concatenate(weights, axis=0)
                classes, sources = [], []
                for px in (0, 1):
                    for py in (0, 1):
                        dx, cx = (px + sx) // 2, (px + sx) % 2
                        dy, cy = (py + sy) // 2, (py + sy) % 2
                        if abs(dx) > 1 or abs(dy) > 1:
                            continue
                        classes.append(px * 2 + py)
                        for z in levels:
                            planes = [
                                spread[cx * 2 + cy, (dy + 1) * 3 + dx + 1, 1 + z + dz] for dz in shifts
                            ]
                            sources.append(jnp.concatenate(planes, axis=1))
                product = jnp.dot(
                    jnp.concatenate(sources, axis=0), weights, preferred_element_type=jnp.float32
                )
                row = 0
                for kind in classes:
                    for z in levels:
                        total[kind, z] += product[row : row + PLANE, :]
                        row += PLANE

    total[...] = jnp.zeros_like(total)
    load_pick.wait()
    for way in ways:
        if way[2] == 0:
            arrive(way)
    for pair in range(4):
        lanes = slice(pair * 256, pair * 256 + 256)
        for corner, (ex, ey) in enumerate(PAIR_WAYS):
            rim[pair, corner * 4 : corner * 4 + 4, :] = thin_rows((ex, ey, 0), pair, 4)
        corners = rim[pair, 0:16, :].astype(jnp.bfloat16)
        for z in range(SIDE_Z):
            spread_plane(
                z + 1, pair, [own[z * PLANE : (z + 1) * PLANE, lanes], face_in[32:96, lanes], face_in[0:32, lanes], corners]
            )
    interact((1, 2))

    for way in ways:
        if way[2] != 0:
            arrive(way)
    for pair in range(4):
        lanes = slice(pair * 256, pair * 256 + 256)
        cx, cy = pair // 2, pair % 2
        for ez in (-1, 1):
            side = 4 + pair * 2 + (ez > 0)
            for number, ey in enumerate((-1, 1)):
                rows = edge_in[PLACES[(0, ey, ez)][1], :, cy * 256 : cy * 256 + 256].astype(jnp.float32)
                rim[side, number * 8 : number * 8 + 8, :] = rows[cx * 8 : cx * 8 + 8, :]
            for number, ex in enumerate((-1, 1)):
                rim[side, 16 + number * 4 : 20 + number * 4, :] = thin_rows((ex, 0, ez), pair, 4)
            for number, (ex, ey) in enumerate(PAIR_WAYS):
                rim[side, 24 + number : 25 + number, :] = thin_rows((ex, ey, ez), pair, 1)
            start = PLACES[(0, 0, ez)][1]
            spread_plane(
                0 if ez < 0 else SIDE_Z + 1, pair,
                [face_in[start : start + PLANE, lanes], rim[side].astype(jnp.bfloat16)],
            )
    interact((0, 3))

    for px in (0, 1):
        for py in (0, 1):
            for pz in (0, 1):
                rows = total[px * 2 + py, :, :, pz * 128 : pz * 128 + 128].reshape(PARENTS, 128)
                field[pl.ds(child_of(px, py, pz), PARENTS, stride=8), :] = rows
    for morton in range(0, PARENTS, 2):
        parts = [field[place * 8 : place * 8 + 8, :] for place in map(parent_place, (morton, morton + 1))]
        out[morton * 8 : morton * 8 + 16, :] = pack(parts)
    for way in ways:

        @pl.when(near[way][0])
        def _():
            copy_to(way).wait_send()


def expand_kernel(expand, reduced, out):
    out[...] = lax.dot_general(
        expand[...], reduced[...], (((1,), (1,)), ((), ())), preferred_element_type=jnp.float32
    )


def local(multipoles, compress, operators, expand):
    cells, rank = multipoles.shape[1], compress.shape[1]
    bit_lists = bits_of_dimension(lax.axis_size("cells"), cells.bit_length() - 1)
    vmem, anywhere = pl.BlockSpec(memory_space=pltpu.VMEM), pl.BlockSpec(memory_space=pl.ANY)
    table = jnp.asarray(picks(), jnp.bfloat16)
    half = jnp.bfloat16
    edges = sum(place[0] == "edge" for place in PLACES.values())
    thins = sum(place[0] == "thin" for place in PLACES.values())
    reduced = pl.pallas_call(
        functools.partial(reduce_kernel, bit_lists),
        out_shape=jax.ShapeDtypeStruct((cells, rank), half),
        in_specs=[anywhere] * 4,
        out_specs=vmem,
        scratch_shapes=[
            pltpu.VMEM(multipoles.shape, half),
            pltpu.VMEM(compress.shape, half),
            pltpu.VMEM(table.shape, half),
            pltpu.VMEM(operators.shape, half),
            pltpu.VMEM((cells, rank), jnp.float32),
            pltpu.VMEM((PARENTS, 8 * rank), half),
            pltpu.VMEM((96, 8 * rank), half),
            pltpu.VMEM((edges, 16, 4 * rank), half),
            pltpu.VMEM((thins, 16, 2 * rank), half),
            pltpu.VMEM((160, 8 * rank), half),
            pltpu.VMEM((edges, 16, 4 * rank), half),
            pltpu.VMEM((thins, 16, 2 * rank), half),
            pltpu.VMEM((12, 32, 2 * rank), jnp.float32),
            pltpu.VMEM((4, 9, SIDE_Z + 2, PLANE, 2 * rank), half),
            pltpu.VMEM((4, SIDE_Z, PLANE, 2 * rank), jnp.float32),
            pltpu.SemaphoreType.DMA((10,)),
            pltpu.SemaphoreType.DMA((len(WAYS),)),
            pltpu.SemaphoreType.DMA((len(WAYS),)),
        ],
        compiler_params=pltpu.CompilerParams(
            collective_id=0, has_side_effects=True, vmem_limit_bytes=48 * 2**20
        ),
        name="interactions",
    )(multipoles, compress, table, operators)
    return pl.pallas_call(
        expand_kernel,
        out_shape=jax.ShapeDtypeStruct((expand.shape[1], cells), jnp.float32),
        in_specs=[vmem] * 2,
        out_specs=vmem,
        compiler_params=pltpu.CompilerParams(vmem_limit_bytes=16 * 2**20),
        name="expansion",
    )(expand.T, reduced)


def solution(mesh):
    placed = (P(None, "cells"), P(), P(), P())
    return jax.shard_map(
        local, mesh=mesh, in_specs=placed, out_specs=P(None, "cells"), check_vma=False
    )
```

time: 35.3 us -> 29.4 us (0.83)
  Pallas kernels: 31.1 us -> 26.2 us
  local copies, waits for them, and re-layouts: 3.84 us -> 3 us
    pallas_call x2, Pallas kernels: 31.1 us -> 26.2 us  [the longest x1 25 us: local(): pl.pallas_call(functools.partial(reduce_kernel, bit_lists), out_shape=jax...]
    unnamed x7 -> x8, local copies, waits for them, and re-layouts: 3.84 us -> 3 us
where the time goes in v1:
time: 29.4 us; the launch traced here: 29.2 us
  Pallas kernels  26.2 us (89%)
  local copies, waits for them, and re-layouts  3 us (10%)
    pallas_call x1, Pallas kernels, local(): pl.pallas_call(functools.partial(reduce_kernel, bit_lists), out_shape=jax...  25 us
    unnamed x8, local copies, waits for them, and re-layouts  3 us
    pallas_call x1, Pallas kernels, local(): pl.pallas_call(expand_kernel, out_shape=jax.ShapeDtypeStruct((expand.shap...  1.2 us

profile of v1, /device:TPU:7, one launch (start us, length us, event | category | flops | bytes accessed | tf_op | source)
XLA Modules:
  0.0 29.2 jit_solution(16938515589578345480)
XLA Ops:
  0.0 0.0 copy-start
  0.0 1.2 %copy-done = bf16[6,288,256]{2,1,0:T(8,128)(2,1)S(1)} copy-done((bf16[6,288,256]{2,1,0:T(8,128)(2,1)S(1)}, bf16[6,288,256]{2,1,0:T(8,128)(2,1)}, u32[]{:S(2)}) %copy-start) | copy-done | bytes 884760
  1.2 0.0 copy-start.1
  1.2 1.0 %copy-done.1 = bf16[216,1024]{1,0:T(8,128)(2,1)S(1)} copy-done((bf16[216,1024]{1,0:T(8,128)(2,1)S(1)}, bf16[216,1024]{1,0:T(8,128)(2,1)}, u32[]{:S(2)}) %copy-start.1) | copy-done | bytes 442392
  2.2 0.0 copy-start.2
  2.2 0.8 %copy-done.2 = bf16[216,128]{1,0:T(8,128)(2,1)S(1)} copy-done((bf16[216,128]{1,0:T(8,128)(2,1)S(1)}, bf16[216,128]{1,0:T(8,128)(2,1)}, u32[]{:S(2)}) %copy-start.2) | copy-done | bytes 55320
  3.0 0.0 copy-start.3
  3.0 25.0 %interactions.1.reduced = bf16[1024,128]{1,0:T(8,128)(2,1)S(1)} custom-call(bf16[216,1024]{1,0:T(8,128)(2,1)S(1)} %copy-done.1, bf16[216,128]{1,0:T(8,128)(2,1)S(1)} %copy-done.2, bf16[6,288,256]{2,1,0:T(8,128)(2,1)S(1)} %copy-done, bf16[316,128,128]{2,1,0:T(8,128)(2,1)} %operators.1), custom_call_target="tpu_custom_call" | custom-call | tf_op jit(solution)/shard_map/interactions/pallas_call | solution.py:365
  28.0 0.0 copy-done.3
  28.0 1.2 %expansion.1 = f32[216,1024]{1,0:T(8,128)} custom-call(bf16[216,128]{1,0:T(8,128)(2,1)S(1)} %bitcast.1, bf16[1024,128]{1,0:T(8,128)(2,1)S(1)} %interactions.1.reduced), custom_call_target="tpu_custom_call" | custom-call | tf_op jit(solution)/shard_map/expansion/pallas_call | solution.py:395
Async XLA Ops:
  0.0 1.2 %copy-start = (bf16[6,288,256]{2,1,0:T(8,128)(2,1)S(1)}, bf16[6,288,256]{2,1,0:T(8,128)(2,1)}, u32[]{:S(2)}) copy-start(bf16[6,288,256]{2,1,0:T(8,128)(2,1)} %constant.2.clone.pick_hbm) | copy-start | bytes 2654212
  1.2 1.0 %copy-start.1 = (bf16[216,1024]{1,0:T(8,128)(2,1)S(1)}, bf16[216,1024]{1,0:T(8,128)(2,1)}, u32[]{:S(2)}) copy-start(bf16[216,1024]{1,0:T(8,128)(2,1)} %multipoles_hbm.1) | copy-start | bytes 1327108
  2.2 0.8 %copy-start.2 = (bf16[216,128]{1,0:T(8,128)(2,1)S(1)}, bf16[216,128]{1,0:T(8,128)(2,1)}, u32[]{:S(2)}) copy-start(bf16[216,128]{1,0:T(8,128)(2,1)} %compress_hbm.1) | copy-start | bytes 165892
  3.0 25.0 %copy-start.3 = (bf16[128,216]{0,1:T(8,128)(2,1)S(1)}, bf16[128,216]{0,1:T(8,128)(2,1)}, u32[]{:S(2)}) copy-start(bf16[128,216]{0,1:T(8,128)(2,1)} %param.8) | copy-start | bytes 165892

commit v2 on v1

--- a/solution.py
+++ b/solution.py
@@ -105,7 +105,7 @@
     load_multipoles.start()
     load_compress.start()
     load_pick.start()
-    for sx in range(-3, 4):
+    for sx in (-2, -1, 0, 1, 2, -3, 3):
         load_operators(sx).start()
 
     me = lax.axis_index("cells")
@@ -255,45 +255,48 @@
     def thin_rows(way, pair, count):
         return thin_in[PLACES[way][1]].astype(jnp.float32)[pair * count : (pair + 1) * count, :]
 
-    def interact(levels):
-        for sx in range(-3, 4):
-            if levels[0] != 0:
-                load_operators(sx).wait()
-            for sy in range(-3, 4):
-                weights, shifts = [], []
-                for dz in (-1, 0, 1):
-                    entries = [
-                        [offsets.get((sx, sy, 2 * dz + cz - pz)) for pz in (0, 1)] for cz in (0, 1)
-                    ]
-                    if all(entry is None for row in entries for entry in row):
-                        continue
-                    blank = jnp.zeros((128, 128), jnp.bfloat16)
-                    for row in entries:
-                        row = [blank if entry is None else held[entry] for entry in row]
-                        weights.append(jnp.concatenate(row, axis=1))
-                    shifts.append(dz)
-                weights = jnp.concatenate(weights, axis=0)
-                classes, sources = [], []
-                for px in (0, 1):
-                    for py in (0, 1):
-                        dx, cx = (px + sx) // 2, (px + sx) % 2
-                        dy, cy = (py + sy) // 2, (py + sy) % 2
-                        if abs(dx) > 1 or abs(dy) > 1:
-                            continue
-                        classes.append(px * 2 + py)
-                        for z in levels:
-                            planes = [
-                                spread[cx * 2 + cy, (dy + 1) * 3 + dx + 1, 1 + z + dz] for dz in shifts
-                            ]
-                            sources.append(jnp.concatenate(planes, axis=1))
-                product = jnp.dot(
-                    jnp.concatenate(sources, axis=0), weights, preferred_element_type=jnp.float32
-                )
-                row = 0
-                for kind in classes:
-                    for z in levels:
-                        total[kind, z] += product[row : row + PLANE, :]
-                        row += PLANE
+    def weights_of(sx, sy):
+        weights, shifts = [], []
+        for dz in (-1, 0, 1):
+            entries = [[offsets.get((sx, sy, 2 * dz + cz - pz)) for pz in (0, 1)] for cz in (0, 1)]
+            if all(entry is None for row in entries for entry in row):
+                continue
+            blank = jnp.zeros((128, 128), jnp.bfloat16)
+            for row in entries:
+                row = [blank if entry is None else held[entry] for entry in row]
+                weights.append(jnp.concatenate(row, axis=1))
+            shifts.append(dz)
+        return weights, shifts
+
+    def interact(levels, group):
+        sx, sy = group[0]
+        classes = [
+            (px, py)
+            for px in (0, 1)
+            for py in (0, 1)
+            if abs((px + sx) // 2) <= 1 and abs((py + sy) // 2) <= 1
+        ]
+        weights, sources = [], {(kind, z): [] for kind in classes for z in levels}
+        for sx, sy in group:
+            tiles, shifts = weights_of(sx, sy)
+            weights += tiles
+            for px, py in classes:
+                dx, cx = (px + sx) // 2, (px + sx) % 2
+                dy, cy = (py + sy) // 2, (py + sy) % 2
+                for z in levels:
+                    for dz in shifts:
+                        plane = spread[cx * 2 + cy, (dy + 1) * 3 + dx + 1, 1 + z + dz]
+                        sources[(px, py), z].append(plane)
+        rows = [jnp.concatenate(planes, axis=1) for planes in sources.values()]
+        product = jnp.dot(
+            jnp.concatenate(rows, axis=0),
+            jnp.concatenate(weights, axis=0),
+            preferred_element_type=jnp.float32,
+        )
+        for number, ((px, py), z) in enumerate(sources):
+            total[px * 2 + py, z] += product[number * PLANE : (number + 1) * PLANE, :]
+
+    middle = range(-2, 3)
 
     total[...] = jnp.zeros_like(total)
     load_pick.wait()
@@ -309,7 +312,9 @@
             spread_plane(
                 z + 1, pair, [own[z * PLANE : (z + 1) * PLANE, lanes], face_in[32:96, lanes], face_in[0:32, lanes], corners]
             )
-    interact((1, 2))
+    for sx in middle:
+        load_operators(sx).wait()
+        interact((1, 2), [(sx, sy) for sy in middle])
 
     for way in ways:
         if way[2] != 0:
@@ -331,7 +336,16 @@
                 0 if ez < 0 else SIDE_Z + 1, pair,
                 [face_in[start : start + PLANE, lanes], rim[side].astype(jnp.bfloat16)],
             )
-    interact((0, 3))
+    for sx in middle:
+        interact((0, 3), [(sx, sy) for sy in middle])
+    levels = range(SIDE_Z)
+    for sx in (-3, 3):
+        load_operators(sx).wait()
+    for far in (-3, 3):
+        interact(levels, [(far, sy) for sy in middle])
+        interact(levels, [(sx, far) for sx in middle])
+        for other in (-3, 3):
+            interact(levels, [(far, other)])
 
     for px in (0, 1):
         for py in (0, 1):
@@ -388,7 +402,7 @@
             pltpu.SemaphoreType.DMA((len(WAYS),)),
         ],
         compiler_params=pltpu.CompilerParams(
-            collective_id=0, has_side_effects=True, vmem_limit_bytes=48 * 2**20
+            collective_id=0, has_side_effects=True, vmem_limit_bytes=62 * 2**20
         ),
         name="interactions",
     )(multipoles, compress, table, operators)

time: 29.4 us -> 25.9 us (0.88)
  local copies, waits for them, and re-layouts: 3 us -> 0.95 us
  Pallas kernels: 26.2 us -> 24.8 us
    unnamed x8 -> x4, local copies, waits for them, and re-layouts: 3 us -> 0.95 us
    pallas_call x1, Pallas kernels: 25 us -> 23.6 us  [local(): pl.pallas_call(functools.partial(reduce_kernel, bit_lists), out_shape=jax...]
where the time goes in v2:
time: 25.9 us; the launch traced here: 25.8 us
  Pallas kernels  24.8 us (96%)
  local copies, waits for them, and re-layouts  0.95 us (4%)
    pallas_call x1, Pallas kernels, local(): pl.pallas_call(functools.partial(reduce_kernel, bit_lists), out_shape=jax...  23.6 us
    pallas_call x1, Pallas kernels, local(): pl.pallas_call(expand_kernel, out_shape=jax.ShapeDtypeStruct((expand.shap...  1.19 us
    unnamed x4, local copies, waits for them, and re-layouts  0.95 us

profile of v2, /device:TPU:7, one launch (start us, length us, event | category | flops | bytes accessed | tf_op | source)
XLA Modules:
  0.0 25.8 jit_solution(13680603273066899832)
XLA Ops:
  0.0 0.0 copy-start.1
  0.0 23.6 %interactions.1.reduced = bf16[1024,128]{1,0:T(8,128)(2,1)} custom-call(bf16[216,1024]{1,0:T(8,128)(2,1)} %multipoles_hbm.1, bf16[216,128]{1,0:T(8,128)(2,1)} %compress_hbm.1, bf16[6,288,256]{2,1,0:T(8,128)(2,1)} %constant.2.clone.pick_hbm, bf16[316,128,128]{2,1,0:T(8,128)(2,1)} %operators.1), custom_call_target="tpu_custom_call" | custom-call | tf_op jit(solution)/shard_map/interactions/pallas_call | solution.py:379
  23.6 0.0 copy-done.1
  23.7 0.0 copy-start
  23.7 0.9 %copy-done = bf16[1024,128]{1,0:T(8,128)(2,1)S(1)} copy-done((bf16[1024,128]{1,0:T(8,128)(2,1)S(1)}, bf16[1024,128]{1,0:T(8,128)(2,1)}, u32[]{:S(2)}) %copy-start) | copy-done | bytes 262168
  24.6 1.2 %expansion.1 = f32[216,1024]{1,0:T(8,128)} custom-call(bf16[216,128]{1,0:T(8,128)(2,1)S(1)} %bitcast.1, bf16[1024,128]{1,0:T(8,128)(2,1)S(1)} %copy-done), custom_call_target="tpu_custom_call" | custom-call | tf_op jit(solution)/shard_map/expansion/pallas_call | solution.py:409
Async XLA Ops:
  0.0 23.6 %copy-start.1 = (bf16[128,216]{0,1:T(8,128)(2,1)S(1)}, bf16[128,216]{0,1:T(8,128)(2,1)}, u32[]{:S(2)}) copy-start(bf16[128,216]{0,1:T(8,128)(2,1)} %param.8) | copy-start | bytes 165892
  23.7 1.0 %copy-start = (bf16[1024,128]{1,0:T(8,128)(2,1)S(1)}, bf16[1024,128]{1,0:T(8,128)(2,1)}, u32[]{:S(2)}) copy-start(bf16[1024,128]{1,0:T(8,128)(2,1)} %interactions.1.reduced) | copy-start | bytes 786436

commit v3 on v2

--- a/solution.py
+++ b/solution.py
@@ -177,31 +177,32 @@
         return jnp.concatenate(parts, axis=0).astype(jnp.bfloat16)
 
     children = [(cx, cy, cz) for cx in (0, 1) for cy in (0, 1) for cz in (0, 1)]
-    for number, bits in enumerate(children):
-        child, lanes = child_of(*bits), slice(number * 128, number * 128 + 128)
-        for z in range(SIDE_Z):
-            own[z * PLANE : (z + 1) * PLANE, lanes] = line(z * PLANE, child, PLANE, 1).astype(jnp.bfloat16)
-        for ex in (-1, 1):
-            start = PLACES[(ex, 0, 0)][1]
-            x = SIDE_X - 1 if ex > 0 else 0
-            face_out[start : start + 16, lanes] = line(x, child, 16, SIDE_X).astype(jnp.bfloat16)
-        for ey in (-1, 1):
-            start = PLACES[(0, ey, 0)][1]
-            y = SIDE_Y - 1 if ey > 0 else 0
-            parts = [line(z * PLANE + y * SIDE_X, child, SIDE_X, 1) for z in range(SIDE_Z)]
-            face_out[start : start + 32, lanes] = pack(parts)
-    for way in WAYS:
-        kind, start, _ = PLACES[way]
+
+    def pack_own(z):
+        for number, bits in enumerate(children):
+            rows = line(z * PLANE, child_of(*bits), PLANE, 1)
+            own[z * PLANE : (z + 1) * PLANE, number * 128 : number * 128 + 128] = rows.astype(jnp.bfloat16)
+
+    def pack_way(way):
+        kind, start, rows = PLACES[way]
         x = SIDE_X - 1 if way[0] > 0 else 0
         y = SIDE_Y - 1 if way[1] > 0 else 0
         z = SIDE_Z - 1 if way[2] > 0 else 0
         place = z * PLANE + y * SIDE_X + x
-        if kind == "edge":
+        if kind == "face":
+            for number, bits in enumerate(children):
+                child = child_of(*bits)
+                if way[0]:
+                    parts = [line(x, child, 16, SIDE_X)]
+                else:
+                    parts = [line(z * PLANE + y * SIDE_X, child, SIDE_X, 1) for z in range(SIDE_Z)]
+                face_out[start : start + rows, number * 128 : number * 128 + 128] = pack(parts)
+        elif kind == "edge":
             for cy in (0, 1):
                 for cz in (0, 1):
                     parts = [line(place, child_of(cx, cy, cz), SIDE_X, 1) for cx in (0, 1)]
                     edge_out[start, :, (cy * 2 + cz) * 128 : (cy * 2 + cz + 1) * 128] = pack(parts)
-        elif kind == "thin":
+        else:
             for cz in (0, 1):
                 parts = []
                 for pair in range(4):
@@ -215,8 +216,6 @@
                 if way[1] and way[2]:
                     parts.append(jnp.zeros((12, 128), jnp.float32))
                 thin_out[start, :, cz * 128 : cz * 128 + 128] = pack(parts)
-
-    pl.semaphore_wait(barrier, peers)
 
     def copy_to(way):
         back = tuple(-step for step in way)
@@ -233,11 +232,28 @@
             device_id_type=pl.DeviceIdType.MESH,
         )
 
-    for way in ways:
-
-        @pl.when(near[way][0])
-        def _():
-            copy_to(way).start()
+    def send(some):
+        for way in some:
+
+            @pl.when(near[way][0])
+            def _():
+                copy_to(way).start()
+
+    flat_ways = [way for way in ways if way[2] == 0]
+    face_ways = [way for way in ways if way[:2] == (0, 0)]
+    slant_ways = [way for way in ways if way[2] != 0 and way not in face_ways]
+    for way in flat_ways:
+        pack_way(way)
+    pl.semaphore_wait(barrier, peers)
+    send(flat_ways)
+    pack_own(0)
+    pack_own(SIDE_Z - 1)
+    send(face_ways)
+    for way in slant_ways:
+        pack_way(way)
+    send(slant_ways)
+    for z in range(1, SIDE_Z - 1):
+        pack_own(z)
 
     def arrive(way):
         @pl.when(near[way][0])
@@ -406,12 +422,17 @@
         ),
         name="interactions",
     )(multipoles, compress, table, operators)
+    columns = cells // 2
     return pl.pallas_call(
         expand_kernel,
         out_shape=jax.ShapeDtypeStruct((expand.shape[1], cells), jnp.float32),
-        in_specs=[vmem] * 2,
-        out_specs=vmem,
-        compiler_params=pltpu.CompilerParams(vmem_limit_bytes=16 * 2**20),
+        grid=(cells // columns,),
+        in_specs=[
+            pl.BlockSpec((expand.shape[1], rank), lambda step: (0, 0)),
+            pl.BlockSpec((columns, rank), lambda step: (step, 0)),
+        ],
+        out_specs=pl.BlockSpec((expand.shape[1], columns), lambda step: (0, step)),
+        compiler_params=pltpu.CompilerParams(vmem_limit_bytes=62 * 2**20),
         name="expansion",
     )(expand.T, reduced)
 

time: 25.9 us -> 25.9 us (level)
  Pallas kernels: 24.8 us -> 25.8 us
  local copies, waits for them, and re-layouts: 0.95 us -> 0 us
    unnamed x4 -> x0, local copies, waits for them, and re-layouts: 0.95 us -> none
    pallas_call x1, Pallas kernels: 1.19 us -> 2.13 us  [local(): pl.pallas_call(expand_kernel, out_shape=jax.ShapeDtypeStruct((expand.shap...]
where the time goes in v3:
time: 25.9 us; the launch traced here: 25.8 us
  Pallas kernels  25.8 us (100%)
    pallas_call x1, Pallas kernels, local(): pl.pallas_call(functools.partial(reduce_kernel, bit_lists), out_shape=jax...  23.6 us
    pallas_call x1, Pallas kernels, local(): pl.pallas_call(expand_kernel, out_shape=jax.ShapeDtypeStruct((expand.shap...  2.13 us

profile of v3, /device:TPU:7, one launch (start us, length us, event | category | flops | bytes accessed | tf_op | source)
XLA Modules:
  0.0 25.8 jit_solution(5527258058538185050)
XLA Ops:
  0.0 23.6 %interactions.1.reduced = bf16[1024,128]{1,0:T(8,128)(2,1)} custom-call(bf16[216,1024]{1,0:T(8,128)(2,1)} %multipoles_hbm.1, bf16[216,128]{1,0:T(8,128)(2,1)} %compress_hbm.1, bf16[6,288,256]{2,1,0:T(8,128)(2,1)} %constant.2.clone.pick_hbm, bf16[316,128,128]{2,1,0:T(8,128)(2,1)} %operators.1), custom_call_target="tpu_custom_call" | custom-call | tf_op jit(solution)/shard_map/interactions/pallas_call | solution.py:395
  23.6 2.1 %expansion.1 = f32[216,1024]{1,0:T(8,128)} custom-call(bf16[216,128]{1,0:T(8,128)(2,1)} %bitcast.1, bf16[1024,128]{1,0:T(8,128)(2,1)} %interactions.1.reduced), custom_call_target="tpu_custom_call" | custom-call | tf_op jit(solution)/shard_map/expansion/pallas_call | solution.py:426

commit v4 on v3

--- a/solution.py
+++ b/solution.py
@@ -328,10 +328,6 @@
             spread_plane(
                 z + 1, pair, [own[z * PLANE : (z + 1) * PLANE, lanes], face_in[32:96, lanes], face_in[0:32, lanes], corners]
             )
-    for sx in middle:
-        load_operators(sx).wait()
-        interact((1, 2), [(sx, sy) for sy in middle])
-
     for way in ways:
         if way[2] != 0:
             arrive(way)
@@ -352,9 +348,10 @@
                 0 if ez < 0 else SIDE_Z + 1, pair,
                 [face_in[start : start + PLANE, lanes], rim[side].astype(jnp.bfloat16)],
             )
+    levels = range(SIDE_Z)
     for sx in middle:
-        interact((0, 3), [(sx, sy) for sy in middle])
-    levels = range(SIDE_Z)
+        load_operators(sx).wait()
+        interact(levels, [(sx, sy) for sy in middle])
     for sx in (-3, 3):
         load_operators(sx).wait()
     for far in (-3, 3):

time: 25.9 us -> 28.7 us (1.11)
  Pallas kernels: 25.8 us -> 28.6 us
    pallas_call x1, Pallas kernels: 23.6 us -> 26.5 us  [local(): pl.pallas_call(functools.partial(reduce_kernel, bit_lists), out_shape=jax...]
where the time goes in v4:
time: 28.7 us; the launch traced here: 28.6 us
  Pallas kernels  28.6 us (100%)
    pallas_call x1, Pallas kernels, local(): pl.pallas_call(functools.partial(reduce_kernel, bit_lists), out_shape=jax...  26.5 us
    pallas_call x1, Pallas kernels, local(): pl.pallas_call(expand_kernel, out_shape=jax.ShapeDtypeStruct((expand.shap...  2.13 us

profile of v4, /device:TPU:7, one launch (start us, length us, event | category | flops | bytes accessed | tf_op | source)
XLA Modules:
  0.0 28.6 jit_solution(15946744522384574485)
XLA Ops:
  0.0 26.5 %interactions.1.reduced = bf16[1024,128]{1,0:T(8,128)(2,1)} custom-call(bf16[216,1024]{1,0:T(8,128)(2,1)} %multipoles_hbm.1, bf16[216,128]{1,0:T(8,128)(2,1)} %compress_hbm.1, bf16[6,288,256]{2,1,0:T(8,128)(2,1)} %constant.2.clone.pick_hbm, bf16[316,128,128]{2,1,0:T(8,128)(2,1)} %operators.1), custom_call_target="tpu_custom_call" | custom-call | tf_op jit(solution)/shard_map/interactions/pallas_call | solution.py:392
  26.5 2.1 %expansion.1 = f32[216,1024]{1,0:T(8,128)} custom-call(bf16[216,128]{1,0:T(8,128)(2,1)} %bitcast.1, bf16[1024,128]{1,0:T(8,128)(2,1)} %interactions.1.reduced), custom_call_target="tpu_custom_call" | custom-call | tf_op jit(solution)/shard_map/expansion/pallas_call | solution.py:423

commit v5 on v4

--- a/solution.py
+++ b/solution.py
@@ -271,20 +271,7 @@
     def thin_rows(way, pair, count):
         return thin_in[PLACES[way][1]].astype(jnp.float32)[pair * count : (pair + 1) * count, :]
 
-    def weights_of(sx, sy):
-        weights, shifts = [], []
-        for dz in (-1, 0, 1):
-            entries = [[offsets.get((sx, sy, 2 * dz + cz - pz)) for pz in (0, 1)] for cz in (0, 1)]
-            if all(entry is None for row in entries for entry in row):
-                continue
-            blank = jnp.zeros((128, 128), jnp.bfloat16)
-            for row in entries:
-                row = [blank if entry is None else held[entry] for entry in row]
-                weights.append(jnp.concatenate(row, axis=1))
-            shifts.append(dz)
-        return weights, shifts
-
-    def interact(levels, group):
+    def interact(work, group):
         sx, sy = group[0]
         classes = [
             (px, py)
@@ -292,25 +279,32 @@
             for py in (0, 1)
             if abs((px + sx) // 2) <= 1 and abs((py + sy) // 2) <= 1
         ]
-        weights, sources = [], {(kind, z): [] for kind in classes for z in levels}
-        for sx, sy in group:
-            tiles, shifts = weights_of(sx, sy)
-            weights += tiles
-            for px, py in classes:
-                dx, cx = (px + sx) // 2, (px + sx) % 2
-                dy, cy = (py + sy) // 2, (py + sy) % 2
-                for z in levels:
-                    for dz in shifts:
+        for dz, levels in work:
+            weights, sources = [], {(kind, z): [] for kind in classes for z in levels}
+            for sx, sy in group:
+                entries = [[offsets.get((sx, sy, 2 * dz + cz - pz)) for pz in (0, 1)] for cz in (0, 1)]
+                if all(entry is None for row in entries for entry in row):
+                    continue
+                blank = jnp.zeros((128, 128), jnp.bfloat16)
+                for row in entries:
+                    row = [blank if entry is None else held[entry] for entry in row]
+                    weights.append(jnp.concatenate(row, axis=1))
+                for px, py in classes:
+                    dx, cx = (px + sx) // 2, (px + sx) % 2
+                    dy, cy = (py + sy) // 2, (py + sy) % 2
+                    for z in levels:
                         plane = spread[cx * 2 + cy, (dy + 1) * 3 + dx + 1, 1 + z + dz]
                         sources[(px, py), z].append(plane)
-        rows = [jnp.concatenate(planes, axis=1) for planes in sources.values()]
-        product = jnp.dot(
-            jnp.concatenate(rows, axis=0),
-            jnp.concatenate(weights, axis=0),
-            preferred_element_type=jnp.float32,
-        )
-        for number, ((px, py), z) in enumerate(sources):
-            total[px * 2 + py, z] += product[number * PLANE : (number + 1) * PLANE, :]
+            if not weights:
+                continue
+            rows = [jnp.concatenate(planes, axis=1) for planes in sources.values()]
+            product = jnp.dot(
+                jnp.concatenate(rows, axis=0),
+                jnp.concatenate(weights, axis=0),
+                preferred_element_type=jnp.float32,
+            )
+            for number, ((px, py), z) in enumerate(sources):
+                total[px * 2 + py, z] += product[number * PLANE : (number + 1) * PLANE, :]
 
     middle = range(-2, 3)
 
@@ -328,6 +322,21 @@
             spread_plane(
                 z + 1, pair, [own[z * PLANE : (z + 1) * PLANE, lanes], face_in[32:96, lanes], face_in[0:32, lanes], corners]
             )
+    groups = [[(sx, sy) for sy in middle] for sx in middle]
+    for far in (-3, 3):
+        groups.append([(far, sy) for sy in middle])
+        groups.append([(sx, far) for sx in middle])
+        groups += [[(far, other)] for other in (-3, 3)]
+    inner = [(0, (0, 1, 2, 3)), (-1, (1, 2, 3)), (1, (0, 1, 2))]
+    outer = [(-1, (0,)), (1, (3,))]
+    for number, group in enumerate(groups):
+        if number < len(middle):
+            load_operators(middle[number]).wait()
+        elif number == len(middle):
+            load_operators(-3).wait()
+            load_operators(3).wait()
+        interact(inner, group)
+
     for way in ways:
         if way[2] != 0:
             arrive(way)
@@ -348,17 +357,8 @@
                 0 if ez < 0 else SIDE_Z + 1, pair,
                 [face_in[start : start + PLANE, lanes], rim[side].astype(jnp.bfloat16)],
             )
-    levels = range(SIDE_Z)
-    for sx in middle:
-        load_operators(sx).wait()
-        interact(levels, [(sx, sy) for sy in middle])
-    for sx in (-3, 3):
-        load_operators(sx).wait()
-    for far in (-3, 3):
-        interact(levels, [(far, sy) for sy in middle])
-        interact(levels, [(sx, far) for sx in middle])
-        for other in (-3, 3):
-            interact(levels, [(far, other)])
+    for group in groups:
+        interact(outer, group)
 
     for px in (0, 1):
         for py in (0, 1):

time: 28.7 us -> 27.2 us (0.948)
  Pallas kernels: 28.6 us -> 27.1 us
    pallas_call x1, Pallas kernels: 26.5 us -> 25 us  [local(): pl.pallas_call(functools.partial(reduce_kernel, bit_lists), out_shape=jax...]
where the time goes in v5:
time: 27.2 us; the launch traced here: 27.1 us
  Pallas kernels  27.1 us (100%)
    pallas_call x1, Pallas kernels, local(): pl.pallas_call(functools.partial(reduce_kernel, bit_lists), out_shape=jax...  25 us
    pallas_call x1, Pallas kernels, local(): pl.pallas_call(expand_kernel, out_shape=jax.ShapeDtypeStruct((expand.shap...  2.14 us

profile of v5, /device:TPU:7, one launch (start us, length us, event | category | flops | bytes accessed | tf_op | source)
XLA Modules:
  0.0 27.1 jit_solution(8962947136556508155)
XLA Ops:
  0.0 25.0 %interactions.1.reduced = bf16[1024,128]{1,0:T(8,128)(2,1)} custom-call(bf16[216,1024]{1,0:T(8,128)(2,1)} %multipoles_hbm.1, bf16[216,128]{1,0:T(8,128)(2,1)} %compress_hbm.1, bf16[6,288,256]{2,1,0:T(8,128)(2,1)} %constant.2.clone.pick_hbm, bf16[316,128,128]{2,1,0:T(8,128)(2,1)} %operators.1), custom_call_target="tpu_custom_call" | custom-call | tf_op jit(solution)/shard_map/interactions/pallas_call | solution.py:392
  25.0 2.1 %expansion.1 = f32[216,1024]{1,0:T(8,128)} custom-call(bf16[216,128]{1,0:T(8,128)(2,1)} %bitcast.1, bf16[1024,128]{1,0:T(8,128)(2,1)} %interactions.1.reduced), custom_call_target="tpu_custom_call" | custom-call | tf_op jit(solution)/shard_map/expansion/pallas_call | solution.py:423

commit v6 on v3

--- a/solution.py
+++ b/solution.py
@@ -376,12 +376,6 @@
         @pl.when(near[way][0])
         def _():
             copy_to(way).wait_send()
-
-
-def expand_kernel(expand, reduced, out):
-    out[...] = lax.dot_general(
-        expand[...], reduced[...], (((1,), (1,)), ((), ())), preferred_element_type=jnp.float32
-    )
 
 
 def local(multipoles, compress, operators, expand):
@@ -422,19 +416,9 @@
         ),
         name="interactions",
     )(multipoles, compress, table, operators)
-    columns = cells // 2
-    return pl.pallas_call(
-        expand_kernel,
-        out_shape=jax.ShapeDtypeStruct((expand.shape[1], cells), jnp.float32),
-        grid=(cells // columns,),
-        in_specs=[
-            pl.BlockSpec((expand.shape[1], rank), lambda step: (0, 0)),
-            pl.BlockSpec((columns, rank), lambda step: (step, 0)),
-        ],
-        out_specs=pl.BlockSpec((expand.shape[1], columns), lambda step: (0, step)),
-        compiler_params=pltpu.CompilerParams(vmem_limit_bytes=62 * 2**20),
-        name="expansion",
-    )(expand.T, reduced)
+    return lax.dot_general(
+        expand, reduced, (((0,), (1,)), ((), ())), preferred_element_type=jnp.float32
+    )
 
 
 def solution(mesh):

time: 25.9 us -> 26 us (level)
  Pallas kernels: 25.8 us -> 23.6 us
  matrix products: 0 us -> 2.19 us
    dot_general x0 -> x1, matrix products: none -> 2.19 us  [local(): lax.dot_general(expand, reduced, (((0,), (1,)), ((), ())), preferred_elem...]
    pallas_call x1 -> x0, Pallas kernels: 2.13 us -> none  [local(): pl.pallas_call(expand_kernel, out_shape=jax.ShapeDtypeStruct((expand.shap...]
where the time goes in v6:
time: 26 us; the launch traced here: 25.8 us
  Pallas kernels  23.6 us (91%)
  matrix products  2.19 us (8%)
    pallas_call x1, Pallas kernels, local(): pl.pallas_call(functools.partial(reduce_kernel, bit_lists), out_shape=jax...  23.6 us
    dot_general x1, matrix products, local(): lax.dot_general(expand, reduced, (((0,), (1,)), ((), ())), preferred_elem...  2.19 us

profile of v6, /device:TPU:7, one launch (start us, length us, event | category | flops | bytes accessed | tf_op | source)
XLA Modules:
  0.0 25.8 jit_solution(13666991262789659394)
XLA Ops:
  0.0 0.0 copy-start
  0.0 23.6 %interactions.1 = bf16[1024,128]{1,0:T(8,128)(2,1)} custom-call(bf16[216,1024]{1,0:T(8,128)(2,1)} %multipoles_hbm.1, bf16[216,128]{1,0:T(8,128)(2,1)} %compress_hbm.1, bf16[6,288,256]{2,1,0:T(8,128)(2,1)} %constant.2.clone.pick_hbm, bf16[316,128,128]{2,1,0:T(8,128)(2,1)} %operators.1), custom_call_target="tpu_custom_call" | custom-call | tf_op jit(solution)/shard_map/interactions/pallas_call | solution.py:389
  23.6 0.0 copy-done
  23.7 2.2 %convolution_bitcast_fusion = f32[216,1024]{1,0:T(8,128)} fusion(bf16[1024,128]{1,0:T(8,128)(2,1)} %interactions.1, bf16[128,216]{0,1:T(8,128)(2,1)S(1)} %copy-done), kind=kOutput, calls=%fused_computation | convolution fusion | flops 56623104 | bytes 1202176 | tf_op jit(solution)/shard_map/dot_general | solution.py:419
Async XLA Ops:
  0.0 23.6 %copy-start = (bf16[128,216]{0,1:T(8,128)(2,1)S(1)}, bf16[128,216]{0,1:T(8,128)(2,1)}, u32[]{:S(2)}) copy-start(bf16[128,216]{0,1:T(8,128)(2,1)} %param.8) | copy-start | bytes 165892
